TPU v7x, 32 devices: a whole 2x2x4 slice. The times are simulated.
32 devices in a mesh: win: 4 (over y, x), row: 2 (over core), col: 4 (over z).
Axes of the slice: x: 2, y: 2, z: 4, core: 2. Of those that a mesh axis runs over, the one named last changes fastest.
Arguments:
- spectra: bfloat16 [2, 8, 6144, 768], P(None, None, ('row', 'col'), 'win'), may hold values from -6 to 6
- gain: float32 [6144], P(('row', 'col')), may hold values from 0.1 to 3
Outputs:
- cross: float32 [2, 8, 6144, 6144], P(None, 'win', 'row', 'col')
All inputs are finite; a program needn't handle non-finite values.
Results may differ from a plain program's by a relative error of at most 0.0038.
Values may be sent and summed in bfloat16 or wider, within the bound.
A program may use at most 256 MiB of HBM per device.

v0:
```python
import jax
import jax.numpy as jnp
from jax import lax
from jax.sharding import PartitionSpec as P


def broadcast(value, axis, source):
    kept = jnp.where(lax.axis_index(axis) == source, value, 0).astype(value.dtype)
    return lax.psum(kept, axis)


def per_device(spectra, gain):
    calibrated = spectra.astype(jnp.float32) * gain[None, None, :, None]
    level = jnp.sqrt(jnp.mean(calibrated * calibrated, axis=(0, 1)))
    white = (calibrated / jnp.maximum(level, 0.5)).astype(jnp.bfloat16)
    regrouped = lax.all_to_all(white, "win", split_axis=1, concat_axis=3, tiled=True)
    windows = regrouped.shape[3]
    rows_block = lax.all_gather(regrouped, "col", axis=2, tiled=True)
    ratio = lax.axis_size("col") // lax.axis_size("row")
    col_width = rows_block.shape[2] // ratio
    col_index = lax.axis_index("col")
    portion = col_index % ratio
    root_row = col_index // ratio
    relayed = broadcast(rows_block, "row", root_row)
    cols_block = lax.dynamic_slice_in_dim(relayed, portion * col_width, col_width, 2)
    left_side = jnp.concatenate([rows_block[0], rows_block[1]], axis=-1)
    right_real = jnp.concatenate([cols_block[0], cols_block[1]], axis=-1)
    right_imag = jnp.concatenate([-cols_block[1], cols_block[0]], axis=-1)
    right_both = jnp.stack([right_real, right_imag])
    stacked = jnp.einsum(
        "fiw,ofjw->ofij", left_side, right_both, preferred_element_type=jnp.float32
    )
    return stacked / jnp.float32(windows)


def solution(mesh):
    in_specs = (P(None, None, ("row", "col"), "win"), P(("row", "col")))
    out_specs = P(None, "win", "row", "col")
    return jax.shard_map(
        per_device, mesh=mesh, in_specs=in_specs, out_specs=out_specs, check_vma=False
    )
```

profile of v0, /device:TPU:0, one launch (start us, length us, event | category | flops | bytes accessed | tf_op | source)
XLA Modules:
  0.0 643.1 jit_solution(993827543162699644)
XLA Ops:
  6.5 0.0 all-gather.2.cloned.1.call-start
  6.5 0.0 copy-start
  6.5 3.8 multiply_reduce_fusion
  10.3 0.2 sqrt_maximum_fusion
  10.5 0.0 copy-done
  10.5 1.9 divide_convert_fusion
  12.5 58.4 %all_to_all.18 = bf16[2,8,768,192]{2,3,0,1:T(8,128)(2,1)S(1)} all-to-all(bf16[2,8,768,192]{2,3,0,1:T(8,128)(2,1)S(1)} %divide_convert_fusion), channel_id=1, replica_groups=mesh['win'=4,'row'=2,'col'=4] {'win'}, dimensions={1} | all-to-all | bytes 9437184 | tf_op jit(solution)/shard_map/all_to_all | solution.py:16
  70.9 2.6 copy.15
  73.5 6.7 %copy.16 = bf16[2,2,768,768]{3,2,1,0:T(8,128)(2,1)} copy(bf16[2,2,768,768]{2,3,1,0:T(8,128)(2,1)} %bitcast.30) | data formatting | bytes 9437184 | tf_op jit(solution)/shard_map/all_to_all | solution.py:16
  80.2 0.0 all-gather.2.cloned.1.call-update
  80.2 0.2 all-reduce.2.cloned.1.call-start
  80.5 321.8 %all-gather.2.cloned.1.call-done = bf16[2,2,3072,768]{3,2,1,0:T(8,128)(2,1)} async-done(((bf16[2,2,768,768]{3,2,1,0:T(8,128)(2,1)}), bf16[2,2,3072,768]{3,2,1,0:T(8,128)(2,1)}) %all-gather.2.cloned.1.call-update) | async-done | bytes 18874384 | tf_op jit(solution)/shard_map/all_gather | solution.py:18
  402.2 16.7 %broadcast_select_fusion = bf16[2,2,3072,768]{3,2,1,0:T(8,128)(2,1)} fusion(bf16[2,2,3072,768]{3,2,1,0:T(8,128)(2,1)} %all-gather.2.cloned.1.call-done, pred[]{:T(512)S(6)} %eq.5), kind=kLoop, calls=%fused_computation.6 | loop fusion | flops 9437184 | bytes 37748736 | tf_op jit(solution)/shard_map/jit(_where)/select_n | solution.py:8
  418.9 0.0 all-reduce.2.cloned.1.call-update
  418.9 16.4 %slice_bitcast_fusion.1 = (bf16[2,3072,768]{2,1,0:T(8,128)(2,1)}, bf16[2,3072,768]{2,1,0:T(8,128)(2,1)}) fusion(bf16[2,2,3072,768]{3,2,1,0:T(8,128)(2,1)} %all-gather.2.cloned.1.call-done), kind=kLoop, calls=%fused_computation.8 | loop fusion | bytes 37748736 | tf_op jit(solution)/shard_map/squeeze | solution.py:26
  435.3 45.7 %all-reduce.2.cloned.1.call-done = bf16[2,2,3072,768]{3,2,1,0:T(8,128)(2,1)} async-done(((bf16[2,2,3072,768]{3,2,1,0:T(8,128)(2,1)}), bf16[2,2,3072,768]{3,2,1,0:T(8,128)(2,1)}) %all-reduce.2.cloned.1.call-update) | async-done | bytes 18874384 | tf_op jit(solution)/shard_map/psum | solution.py:9
  481.0 2.6 dynamic-slice_bitcast_fusion.1
  483.6 3.6 fusion.4
  487.2 7.0 %maximum_bitcast_fusion.2 = (bf16[1,2,1536,1536]{3,2,1,0:T(8,128)(2,1)}, bf16[1,2,1536,1536]{3,2,1,0:T(8,128)(2,1)}) fusion(bf16[2,1536,768]{2,1,0:T(8,128)(2,1)S(1)} %get-tuple-element.6, bf16[2,1536,768]{2,1,0:T(8,128)(2,1)S(1)} %dynamic-slice_bitcast_fusion.1, bf16[2,1536,768]{2,1,0:T(8,128)(2,1)S(1)} %get-tuple-element.5), kind=kLoop, calls=%fused_computation.9 | loop fusion | flops 37748736 | bytes 33030144 | tf_op jit(solution)/shard_map/stack | solution.py:29
  494.2 69.0 %multiply_bitcast_fusion = f32[2,2,3072,1536]{2,3,0,1:T(8,128)} fusion(bf16[2,3072,768]{2,1,0:T(8,128)(2,1)} %get-tuple-element.8, bf16[2,3072,768]{2,1,0:T(8,128)(2,1)} %get-tuple-element.7, bf16[1,2,1536,1536]{3,2,1,0:T(8,128)(2,1)} %get-tuple-element.10, bf16[1,2,1536,1536]{3,2,1,0:T(8,128)(2,1)} %get-tuple-element.9), kind=kOutput, calls=%fused_computation | convolution fusion | flops 58048118784 | bytes 113246208 | tf_op jit(solution)/shard_map/fiw,ofjw->ofij/dot_general | solution.py:30
  563.2 73.1 %copy.18 = f32[2,2,3072,1536]{3,2,1,0:T(8,128)} copy(f32[2,2,3072,1536]{2,3,0,1:T(8,128)} %multiply_bitcast_fusion) | data formatting | bytes 150994944 | tf_op jit(solution)/shard_map/div | solution.py:33
Async XLA Ops:
  6.5 395.7 %all-gather.2.cloned.1.call-start = ((), (), s32[]{:S(2)}) async-start(), calls=%async_computation.1 | async-start | bytes 23592960 | tf_op jit(solution)/shard_map/all_gather | solution.py:18
  6.5 4.0 copy-start
  80.2 400.8 %all-reduce.2.cloned.1.call-start = ((), (), s32[]{:S(2)}) async-start(), calls=%async_computation.2 | async-start | bytes 37748736 | tf_op jit(solution)/shard_map/psum | solution.py:9
Sparse Core Ops, SparseCore 0:
  80.3 321.8 all-gather.1
  419.1 61.8 all-reduce.1
where the time goes:
time: 645 us; the launch traced here: 643 us
  waiting for transfers between devices  367 us (57%)
  local copies, waits for them, and re-layouts  101 us (16%)
  matrix products  69 us (11%)
  blocking collectives  58.4 us (9%)
  other arithmetic  33.1 us (5%)
  between operations  13.5 us (2%)
    all_gather x1, waiting for transfers between devices, per_device(): rows_block = lax.all_gather(regrouped, 'col', axis=2, tiled=True)  322 us
    div x1, local copies, waits for them, and re-layouts, per_device(): return stacked / jnp.float32(windows)  73.1 us
    dot_general x1, matrix products, per_device(): jnp.einsum('fiw,ofjw->ofij', left_side, right_both, preferred_element_typ...  69 us
    all_to_all x1, blocking collectives, per_device(): lax.all_to_all(white, 'win', split_axis=1, concat_axis=3, tiled=True)  58.4 us
    psum x1, waiting for transfers between devices, broadcast(): return lax.psum(kept, axis)  45.7 us
    select_n x1, other arithmetic, broadcast(): jnp.where(lax.axis_index(axis) == source, value, 0).astype(value.dtype)  16.7 us
    squeeze x1, local copies, waits for them, and re-layouts, per_device(): left_side = jnp.concatenate([rows_block[0], rows_block[1]], axis=-1)  16.4 us
  transfers between devices with their start and end apart: 2, of which 2 were waited for; matrix products, arithmetic and copies ran while one was open for 3% of the time, Pallas kernels for 0%

commit v1 on v0

--- a/solution.py
+++ b/solution.py
@@ -15,7 +15,21 @@
     white = (calibrated / jnp.maximum(level, 0.5)).astype(jnp.bfloat16)
     regrouped = lax.all_to_all(white, "win", split_axis=1, concat_axis=3, tiled=True)
     windows = regrouped.shape[3]
-    rows_block = lax.all_gather(regrouped, "col", axis=2, tiled=True)
+    ways, here, step = (lax.axis_size("col"), lax.axis_index("col"), regrouped.shape[2])
+    shape = [n * ways if d == 2 else n for d, n in enumerate(regrouped.shape)]
+    full = lax.dynamic_update_slice_in_dim(
+        jnp.zeros(shape, regrouped.dtype), regrouped, here * step, axis=2
+    )
+    going_up = going_down = regrouped
+    for far in range(1, ways // 2 + 1):
+        going_up = lax.ppermute(going_up, "col", [(d, (d + 1) % ways) for d in range(ways)])
+        full = lax.dynamic_update_slice_in_dim(full, going_up, (here - far) % ways * step, axis=2)
+        if 2 * far < ways:
+            going_down = lax.ppermute(going_down, "col", [(d, (d - 1) % ways) for d in range(ways)])
+            full = lax.dynamic_update_slice_in_dim(
+                full, going_down, (here + far) % ways * step, axis=2
+            )
+    rows_block = full
     ratio = lax.axis_size("col") // lax.axis_size("row")
     col_width = rows_block.shape[2] // ratio
     col_index = lax.axis_index("col")

time: 645 us -> 630 us (0.977)
  waiting for transfers between devices: 367 us -> 243 us
  starting transfers between devices: 0.22 us -> 100 us
  local copies, waits for them, and re-layouts: 101 us -> 120 us
  other arithmetic: 33.1 us -> 24.2 us
    all_gather x1 -> x0, waiting for transfers between devices: 322 us -> none  [per_device(): rows_block = lax.all_gather(regrouped, 'col', axis=2, tiled=True)]
    ppermute x0 -> x3, waiting for transfers between devices: none -> 198 us  [the longest x2 198 us: per_device(): lax.ppermute(going_up, 'col', [(d, (d + 1) % ways) for d in range(ways)])]
    ppermute x0 -> x3, starting transfers between devices: none -> 100 us  [the longest x2 98 us: per_device(): lax.ppermute(going_up, 'col', [(d, (d + 1) % ways) for d in range(ways)])]
    dynamic_update_slice x0 -> x4, local copies, waits for them, and re-layouts: none -> 9.23 us  [the longest x2 5.78 us: per_device(): lax.dynamic_update_slice_in_dim(full, going_up, (here - far) % ways * ste...]
    select_n x1, other arithmetic: 16.7 us -> 7.73 us  [broadcast(): jnp.where(lax.axis_index(axis) == source, value, 0).astype(value.dtype)]
    unnamed x2 -> x6, local copies, waits for them, and re-layouts: 0.01 us -> 7.83 us
  transfers between devices with their start and end apart: 2 -> 4, of which waited for: 2 -> 3; matrix products, arithmetic and copies ran while one was open for 3% -> 4% of each run, Pallas kernels for 0% -> 0%
where the time goes in v1:
time: 630 us; the launch traced here: 628 us
  waiting for transfers between devices  243 us (39%)
  local copies, waits for them, and re-layouts  120 us (19%)
  starting transfers between devices  100 us (16%)
  matrix products  68.9 us (11%)
  blocking collectives  58.4 us (9%)
  other arithmetic  24.2 us (4%)
  between operations  13.5 us (2%)
    ppermute x2, waiting for transfers between devices, per_device(): lax.ppermute(going_up, 'col', [(d, (d + 1) % ways) for d in range(ways)])  198 us
    ppermute x2, starting transfers between devices, per_device(): lax.ppermute(going_up, 'col', [(d, (d + 1) % ways) for d in range(ways)])  98 us
    div x1, local copies, waits for them, and re-layouts, per_device(): return stacked / jnp.float32(windows)  73.1 us
    dot_general x1, matrix products, per_device(): jnp.einsum('fiw,ofjw->ofij', left_side, right_both, preferred_element_typ...  68.9 us
    all_to_all x1, blocking collectives, per_device(): lax.all_to_all(white, 'win', split_axis=1, concat_axis=3, tiled=True)  58.4 us
    psum x1, waiting for transfers between devices, broadcast(): return lax.psum(kept, axis)  45.7 us
    squeeze x1, local copies, waits for them, and re-layouts, per_device(): left_side = jnp.concatenate([rows_block[0], rows_block[1]], axis=-1)  16.3 us
  transfers between devices with their start and end apart: 4, of which 3 were waited for; matrix products, arithmetic and copies ran while one was open for 4% of the time, Pallas kernels for 0%

profile of v1, /device:TPU:0, one launch (start us, length us, event | category | flops | bytes accessed | tf_op | source)
XLA Modules:
  0.0 628.1 jit_solution(16865635126119434472)
XLA Ops:
  6.5 0.0 all-reduce.2.cloned.1.call-start
  6.5 0.0 copy-start.1
  6.5 3.8 multiply_reduce_fusion
  10.3 0.2 sqrt_maximum_fusion
  10.5 0.0 copy-done.1
  10.5 1.9 divide_convert_fusion
  12.5 58.4 %all_to_all.18 = bf16[2,8,768,192]{2,3,0,1:T(8,128)(2,1)S(1)} all-to-all(bf16[2,8,768,192]{2,3,0,1:T(8,128)(2,1)S(1)} %divide_convert_fusion), channel_id=1, replica_groups=mesh['win'=4,'row'=2,'col'=4] {'win'}, dimensions={1} | all-to-all | bytes 9437184 | tf_op jit(solution)/shard_map/all_to_all | solution.py:16
  70.9 2.6 copy.19
  73.5 6.7 %copy.20 = bf16[2,2,768,768]{3,2,1,0:T(8,128)(2,1)} copy(bf16[2,2,768,768]{2,3,1,0:T(8,128)(2,1)} %bitcast.30) | data formatting | bytes 9437184 | tf_op jit(solution)/shard_map/all_to_all | solution.py:16
  80.2 1.6 collective-permute-start
  81.7 2.2 collective-permute-start.1
  84.0 103.0 %collective-permute-done = bf16[2,2,768,768]{3,2,1,0:T(8,128)(2,1)} collective-permute-done((bf16[2,2,768,768]{3,2,1,0:T(8,128)(2,1)}, bf16[2,2,768,768]{3,2,1,0:T(8,128)(2,1)}, u32[]{:S(2)}, u32[]{:S(2)}) %collective-permute-start) | collective-permute-done | bytes 4718624 | tf_op jit(solution)/shard_map/ppermute | solution.py:25
  187.0 96.4 %collective-permute-start.2 = (bf16[2,2,768,768]{3,2,1,0:T(8,128)(2,1)}, bf16[2,2,768,768]{3,2,1,0:T(8,128)(2,1)}, u32[]{:S(2)}, u32[]{:S(2)}) collective-permute-start(bf16[2,2,768,768]{3,2,1,0:T(8,128)(2,1)} %collective-permute-done), channel_id=1, source_target_pairs={{0,1},{1,2},{2,3},{3,0},{4,5},{5,6},{6,7},{7,4},{8,9},{9,10},{10,1... | collective-permute-start | bytes 14155784 | tf_op jit(solution)/shard_map/ppermute | solution.py:25
  283.4 1.3 broadcast_in_dim.3
  284.8 1.0 copy-done.2
  285.8 0.6 constant_dynamic-update-slice_fusion.3
  286.3 2.9 constant_dynamic-update-slice_fusion.2
  289.2 0.0 collective-permute-done.1
  289.2 2.9 constant_dynamic-update-slice_fusion.1
  292.1 94.5 %collective-permute-done.2 = bf16[2,2,768,768]{3,2,1,0:T(8,128)(2,1)} collective-permute-done((bf16[2,2,768,768]{3,2,1,0:T(8,128)(2,1)}, bf16[2,2,768,768]{3,2,1,0:T(8,128)(2,1)}, u32[]{:S(2)}, u32[]{:S(2)}) %collective-permute-start.2) | collective-permute-done | bytes 4718624 | tf_op jit(solution)/shard_map/ppermute | solution.py:25
  386.6 2.9 constant_dynamic-update-slice_fusion
  389.5 0.0 copy-start
  389.5 6.8 %copy-done = bf16[2,2,3072,768]{3,2,1,0:T(8,128)(2,1)} copy-done((bf16[2,2,3072,768]{3,2,1,0:T(8,128)(2,1)}, bf16[2,2,3072,768]{3,2,1,0:T(8,128)(2,1)S(1)}, u32[]{:S(2)}) %copy-start) | copy-done | bytes 18874392
  396.4 7.7 %broadcast_select_fusion = bf16[2,2,3072,768]{3,2,1,0:T(8,128)(2,1)} fusion(bf16[2,2,3072,768]{3,2,1,0:T(8,128)(2,1)S(1)} %constant_dynamic-update-slice_fusion, pred[]{:T(512)S(6)} %eq.8), kind=kLoop, calls=%fused_computation.6 | loop fusion | flops 9437184 | bytes 37748736 | tf_op jit(solution)/shard_map/jit(_where)/select_n | solution.py:8
  404.1 0.0 all-reduce.2.cloned.1.call-update
  404.1 16.3 %slice_bitcast_fusion.1 = (bf16[2,3072,768]{2,1,0:T(8,128)(2,1)}, bf16[2,3072,768]{2,1,0:T(8,128)(2,1)}) fusion(bf16[2,2,3072,768]{3,2,1,0:T(8,128)(2,1)} %copy-done), kind=kLoop, calls=%fused_computation.8 | loop fusion | bytes 37748736 | tf_op jit(solution)/shard_map/squeeze | solution.py:40
  420.5 45.7 %all-reduce.2.cloned.1.call-done = bf16[2,2,3072,768]{3,2,1,0:T(8,128)(2,1)} async-done(((bf16[2,2,3072,768]{3,2,1,0:T(8,128)(2,1)}), bf16[2,2,3072,768]{3,2,1,0:T(8,128)(2,1)}) %all-reduce.2.cloned.1.call-update) | async-done | bytes 18874384 | tf_op jit(solution)/shard_map/psum | solution.py:9
  466.2 2.6 dynamic-slice_bitcast_fusion.1
  468.8 3.6 fusion.4
  472.4 6.9 %maximum_bitcast_fusion.2 = (bf16[1,2,1536,1536]{3,2,1,0:T(8,128)(2,1)}, bf16[1,2,1536,1536]{3,2,1,0:T(8,128)(2,1)}) fusion(bf16[2,1536,768]{2,1,0:T(8,128)(2,1)S(1)} %get-tuple-element.6, bf16[2,1536,768]{2,1,0:T(8,128)(2,1)S(1)} %dynamic-slice_bitcast_fusion.1, bf16[2,1536,768]{2,1,0:T(8,128)(2,1)S(1)} %get-tuple-element.5), kind=kLoop, calls=%fused_computation.9 | loop fusion | flops 37748736 | bytes 33030144 | tf_op jit(solution)/shard_map/stack | solution.py:43
  479.4 68.9 %multiply_bitcast_fusion = f32[2,2,3072,1536]{2,3,0,1:T(8,128)} fusion(bf16[2,3072,768]{2,1,0:T(8,128)(2,1)} %get-tuple-element.8, bf16[2,3072,768]{2,1,0:T(8,128)(2,1)} %get-tuple-element.7, bf16[1,2,1536,1536]{3,2,1,0:T(8,128)(2,1)} %get-tuple-element.10, bf16[1,2,1536,1536]{3,2,1,0:T(8,128)(2,1)} %get-tuple-element.9), kind=kOutput, calls=%fused_computation | convolution fusion | flops 58048118784 | bytes 113246208 | tf_op jit(solution)/shard_map/fiw,ofjw->ofij/dot_general | solution.py:44
  548.2 73.1 %copy.24 = f32[2,2,3072,1536]{3,2,1,0:T(8,128)} copy(f32[2,2,3072,1536]{2,3,0,1:T(8,128)} %multiply_bitcast_fusion) | data formatting | bytes 150994944 | tf_op jit(solution)/shard_map/div | solution.py:47
  (1 shorter events, 0.0 us)
Async XLA Ops:
  6.5 459.6 %all-reduce.2.cloned.1.call-start = ((), (), s32[]{:S(2)}) async-start(), calls=%async_computation.1 | async-start | bytes 37748736 | tf_op jit(solution)/shard_map/psum | solution.py:9
  6.5 4.0 copy-start.1
  80.2 106.9 %collective-permute-start = (bf16[2,2,768,768]{3,2,1,0:T(8,128)(2,1)}, bf16[2,2,768,768]{3,2,1,0:T(8,128)(2,1)}, u32[]{:S(2)}, u32[]{:S(2)}) collective-permute-start(bf16[2,2,768,768]{3,2,1,0:T(8,128)(2,1)} %copy.20), channel_id=1, source_target_pairs={{0,1},{1,2},{2,3},{3,0},{4,5},{5,6},{6,7},{7,4},{8,9},{9,10},{10,1... | collective-permute-start | bytes 14155784 | tf_op jit(solution)/shard_map/ppermute | solution.py:25
  81.7 207.5 %collective-permute-start.1 = (bf16[2,2,768,768]{3,2,1,0:T(8,128)(2,1)}, bf16[2,2,768,768]{3,2,1,0:T(8,128)(2,1)}, u32[]{:S(2)}, u32[]{:S(2)}) collective-permute-start(bf16[2,2,768,768]{3,2,1,0:T(8,128)(2,1)} %copy.20), channel_id=1, source_target_pairs={{0,3},{1,0},{2,1},{3,2},{4,7},{5,4},{6,5},{7,6},{8,11},{9,8},{10,9... | collective-permute-start | bytes 14155784 | tf_op jit(solution)/shard_map/ppermute | solution.py:28
  187.0 199.6 %collective-permute-start.2 = (bf16[2,2,768,768]{3,2,1,0:T(8,128)(2,1)}, bf16[2,2,768,768]{3,2,1,0:T(8,128)(2,1)}, u32[]{:S(2)}, u32[]{:S(2)}) collective-permute-start(bf16[2,2,768,768]{3,2,1,0:T(8,128)(2,1)} %collective-permute-done), channel_id=1, source_target_pairs={{0,1},{1,2},{2,3},{3,0},{4,5},{5,6},{6,7},{7,4},{8,9},{9,10},{10,1... | collective-permute-start | bytes 14155784 | tf_op jit(solution)/shard_map/ppermute | solution.py:25
  283.4 2.3 copy-start.2
  389.5 6.9 %copy-start = (bf16[2,2,3072,768]{3,2,1,0:T(8,128)(2,1)}, bf16[2,2,3072,768]{3,2,1,0:T(8,128)(2,1)S(1)}, u32[]{:S(2)}) copy-start(bf16[2,2,3072,768]{3,2,1,0:T(8,128)(2,1)S(1)} %constant_dynamic-update-slice_fusion) | copy-start | bytes 56623108
Sparse Core Ops, SparseCore 0:
  404.2 61.8 all-reduce.1
